TPU v7x, 32 devices: a whole 2x2x4 slice. The times are simulated.
32 devices in a mesh: space: 8 (over z, y), field: 4 (over x, core).
Axes of the slice: x: 2, y: 2, z: 4, core: 2. Of those that a mesh axis runs over, the one named last changes fastest.
Arguments:
- fields: float32 [16, 256, 6144], P('field', 'space'), may hold values from -6 to 6
- zone_ids: int32 [256, 6144], P('space'), may hold values from 0 to 7
- diffusivity: float32 [16, 8], P('field'), may hold values from 0.3 to 3
- heat_rate: float32 [15], replicated, may hold values from 0.3 to 1.5
- weight_in: bfloat16 [384, 16], replicated, may hold values from -1.5 to 1.5
- bias_in: float32 [384], replicated, may hold values from -3 to 3
- weight_mid: bfloat16 [384, 384], replicated, may hold values from -0.3125 to 0.3125
- bias_mid: float32 [384], replicated, may hold values from -3 to 3
- weight_out: bfloat16 [16, 384], replicated, may hold values from -0.3125 to 0.3125
- bias_out: float32 [16], replicated, may hold values from -2 to 2
Outputs:
- new_fields: float32 [16, 256, 6144], P('field', 'space')
All inputs are finite; a program needn't handle non-finite values.
Results may differ from a plain program's by a relative error of at most 0.005.
Values may be sent and summed in bfloat16 or wider, within the bound.
A program may use at most 64 MiB of HBM per device.

v0:
```python
import functools

import jax
import jax.numpy as jnp
from jax import lax
from jax.experimental import pallas as pl
from jax.experimental.pallas import tpu as pltpu
from jax.sharding import PartitionSpec as P

FIELDS = 16
SWEEPS = 3
HALO = 3
SUB = 8
PAIR = 16
STEP = 256
RELAX_WEIGHTS = (0.8, 1.25, 0.95)
MESH = pl.DeviceIdType.MESH
F32 = jnp.float32
BF16 = jnp.bfloat16


def block_lanes(width):
    return 512 if width % 512 == 0 else 256


def iota2(shape, axis):
    return lax.broadcasted_iota(jnp.int32, shape, axis)


def three_rows(row):
    row = row.reshape(1, -1)
    high = row.astype(BF16).astype(F32)
    rest = row - high
    mid = rest.astype(BF16).astype(F32)
    low = rest - mid
    index = iota2((PAIR, row.shape[1]), 0)
    zero = jnp.zeros((PAIR, row.shape[1]), F32)
    out = jnp.where(index == 0, high, zero)
    out = jnp.where(index == 1, mid, out)
    out = jnp.where(index == 2, low, out)
    return out.astype(BF16)


def across(rows16, select):
    return lax.dot_general(rows16, select, (((0,), (0,)), ((), ())), preferred_element_type=F32)


def halves_silu(pre):
    y = pre.astype(BF16)
    return y + y * jnp.tanh(y)


def kernel(
    n,
    n_space,
    fields,
    zones,
    diff,
    rate,
    w_in,
    b_in,
    w_mid,
    b_mid,
    w_out,
    b_out,
    out,
    src,
    coef,
    face_d,
    face_e,
    rdiag,
    s1,
    s2,
    s3,
    halo_out,
    halo_in,
    sbuf,
    xbuf,
    rbuf,
    ret,
    w1,
    w2,
    w3,
    rate_row,
    rate_col,
    halo_ssem,
    halo_rsem,
    ssem,
    rsem,
    rssem,
    rrsem,
    lsem,
    rlsem,
):
    per, rows, columns = fields.shape
    parts = SUB // per
    width = columns // parts
    variants = 2 * parts
    lanes_at_once = block_lanes(width)
    hid = w_mid.shape[0]
    chunks = rows // (2 * n)
    chunk_rows = rows // chunks
    groups = rows // SUB
    here = lax.axis_index("space")
    me = lax.axis_index("field")
    has_up = here > 0
    has_down = here < n_space - 1

    barrier = pltpu.get_barrier_semaphore()
    for off in range(1, n):
        pl.semaphore_signal(
            barrier, inc=1, device_id={"field": lax.rem(me + off, n)}, device_id_type=MESH
        )

    @pl.when(has_up)
    def _():
        pl.semaphore_signal(barrier, inc=1, device_id={"space": here - 1}, device_id_type=MESH)

    @pl.when(has_down)
    def _():
        pl.semaphore_signal(barrier, inc=1, device_id={"space": here + 1}, device_id_type=MESH)

    def prep(g):
        row0 = pl.multiple_of(g * SUB, SUB)
        there = pl.ds(pl.multiple_of((row0 + HALO) * SUB, SUB), SUB * SUB)

        def lane_block(j, carry):
            at = pl.multiple_of(j * STEP, STEP)
            coefs, values = [], []
            for p in range(parts):
                cols = pl.ds(pl.multiple_of(at + p * width, STEP), STEP)
                zone = zones[pl.ds(row0, SUB), cols]
                for f in range(per):
                    value = jnp.full(zone.shape, diff[f, 0], F32)
                    for z in range(1, diff.shape[1]):
                        value = jnp.where(zone == z, diff[f, z], value)
                    coefs.append(value)
                    values.append(fields[f, pl.ds(row0, SUB), cols])
            for buf, made in ((coef, coefs), (src, values)):
                turned = jnp.swapaxes(jnp.stack(made, 0), 0, 1)
                buf[there, pl.ds(at, STEP)] = turned.reshape(SUB * SUB, STEP)
            return carry

        lax.fori_loop(0, width // STEP, lane_block, 0)

    def prep_end(i, carry):
        prep(i * (groups - 1))
        return carry

    lax.fori_loop(0, 2, prep_end, 0)
    top = HALO * SUB
    for side, row in ((0, HALO), (1, rows)):
        halo_out[side] = jnp.concatenate(
            [src[row * SUB : row * SUB + top, :], coef[row * SUB : row * SUB + top, :]], 0
        ).astype(BF16)
    heard = (n - 1) + has_up.astype(jnp.int32) + has_down.astype(jnp.int32)
    pl.semaphore_wait(barrier, heard)

    def halo_copy(side):
        target = here - 1 if side == 0 else here + 1
        return pltpu.make_async_remote_copy(
            src_ref=halo_out.at[side],
            dst_ref=halo_in.at[1 - side],
            send_sem=halo_ssem.at[side],
            recv_sem=halo_rsem.at[1 - side],
            device_id={"space": target},
            device_id_type=MESH,
        )

    @pl.when(has_up)
    def _():
        halo_copy(0).start()

    @pl.when(has_down)
    def _():
        halo_copy(1).start()

    def prep_mid(g, carry):
        prep(g)
        return carry

    lax.fori_loop(1, groups - 1, prep_mid, 0)

    lane0 = iota2((SUB, 128), 1) == 0
    lane_last = iota2((SUB, 128), 1) == 127

    def from_east(x):
        rolled = pltpu.roll(x, width - 1, 1)
        tail = rolled[:, width - 128 :]
        tail = jnp.where(lane_last, pltpu.roll(tail, SUB - per, 0), tail)
        return jnp.concatenate([rolled[:, : width - 128], tail], 1)

    def from_west(x):
        rolled = pltpu.roll(x, 1, 1)
        head = rolled[:, :128]
        head = jnp.where(lane0, pltpu.roll(head, per, 0), head)
        return jnp.concatenate([head, rolled[:, 128:]], 1)

    def at_row(r):
        return pl.ds(pl.multiple_of(r * SUB, SUB), SUB)

    def first_row(r, carry):
        a, b, c = at_row(r - 1), at_row(r), at_row(r + 1)
        mine = coef[b, :]
        down = 0.5 * (mine + coef[c, :])
        up = 0.5 * (mine + coef[a, :])
        east = 0.5 * (mine + from_east(mine))
        west = from_west(east)
        outside = jnp.logical_or(
            jnp.logical_and(r < HALO, jnp.logical_not(has_up)),
            jnp.logical_and(r >= rows + HALO, jnp.logical_not(has_down)),
        )
        scale = jnp.where(outside, 0.0, 1.0).astype(F32)
        inv = scale / (1.0 + down + up + east + west)
        face_d[b, :] = down
        face_e[b, :] = east
        rdiag[b, :] = inv
        v = src[b, :]
        total = v + down * src[c, :] + up * src[a, :]
        total = total + east * from_east(v) + from_west(east * v)
        weight = RELAX_WEIGHTS[0]
        s1[b, :] = (1.0 - weight) * v + (weight * inv) * total
        return carry

    def later_row(old, new, weight, r, carry):
        a, b, c = at_row(r - 1), at_row(r), at_row(r + 1)
        v = old[b, :]
        east = face_e[b, :]
        total = src[b, :] + face_d[b, :] * old[c, :] + face_d[a, :] * old[a, :]
        total = total + east * from_east(v) + from_west(east * v)
        new[b, :] = (1.0 - weight) * v + (weight * rdiag[b, :]) * total
        return carry

    steps = (
        first_row,
        functools.partial(later_row, s1, s2, RELAX_WEIGHTS[1]),
        functools.partial(later_row, s2, s3, RELAX_WEIGHTS[2]),
    )
    done = [set() for _ in steps]

    def stencil(k):
        low, high = k * chunk_rows + HALO, (k + 1) * chunk_rows + HALO
        for number, step in enumerate(steps):
            grow = SWEEPS - 1 - number
            need = sorted(set(range(low - grow, high + grow)) - done[number])
            done[number].update(need)
            lax.fori_loop(need[0], need[-1] + 1, step, 0)
        for d in range(n):
            row = (low + 2 * d) * SUB
            sbuf[k, d] = s3[row : row + PAIR, :].astype(BF16)
        for c in sends(k):
            c.start()

    def all_copies(src_buf, dst_buf, k, send_sem, recv_sem, local_sem):
        copies = []
        for off in range(1, n):
            peer = lax.rem(me + off, n)
            copies.append(
                pltpu.make_async_remote_copy(
                    src_ref=src_buf.at[k, peer],
                    dst_ref=dst_buf.at[k, me],
                    send_sem=send_sem.at[k, off],
                    recv_sem=recv_sem.at[k, off],
                    device_id={"field": peer},
                    device_id_type=MESH,
                )
            )
        local = pltpu.make_async_copy(src_buf.at[k, me], dst_buf.at[k, me], local_sem.at[k])
        return copies + [local]

    def sends(k):
        return all_copies(sbuf, xbuf, k, ssem, rsem, lsem)

    def returns(k):
        return all_copies(rbuf, ret, k, rssem, rrsem, rlsem)

    def halo_wait():
        for slot, row, has in ((0, 0, has_up), (1, rows + HALO, has_down)):
            there = pl.ds(row * SUB, top)

            @pl.when(has)
            def _():
                copy = halo_copy(1 - slot)
                copy.wait_recv()
                both = halo_in[slot].astype(F32)
                src[there, :] = both[:top]
                coef[there, :] = both[top:]

            @pl.when(jnp.logical_not(has))
            def _():
                src[there, :] = jnp.zeros((top, width), F32)
                coef[there, :] = jnp.zeros((top, width), F32)

        @pl.when(has_up)
        def _():
            halo_copy(0).wait_send()

        @pl.when(has_down)
        def _():
            halo_copy(1).wait_send()

    def weights():
        depth = (n + 1) * PAIR
        bias = three_rows(0.5 * b_in[...])
        row, col = iota2((PAIR, depth), 0), iota2((PAIR, depth), 1)
        bias_cols = across(bias, (col == row + n * PAIR).astype(BF16))
        for v in range(variants):
            place = (row // per) * PAIR + v * per + lax.rem(row, per)
            pick = jnp.where(col == place, 0.5, 0.0).astype(BF16)
            spread = across(w_in[...], pick)
            w1[v * hid : (v + 1) * hid, :] = (spread + bias_cols).astype(BF16)
        square = (iota2((PAIR, PAIR), 0) == iota2((PAIR, PAIR), 1)).astype(BF16)
        w2[:, :hid] = w_mid[...] * jnp.asarray(0.5, BF16)
        w2[:, hid:] = across(three_rows(0.5 * b_mid[...]), square).astype(BF16)
        w3[:, :hid] = w_out[...]
        w3[:, hid:] = across(three_rows(b_out[...]), square).astype(BF16)
        rate_row[...] = jnp.zeros(rate_row.shape, F32)
        rate_row[0:1, 0 : FIELDS - 1] = rate[...].reshape(1, FIELDS - 1)
        ones = jnp.ones((PAIR, lanes_at_once), BF16)
        rate_col[...] = across(three_rows(rate_row[0:1, :])[:, :FIELDS], ones)
        for k in range(chunks):
            xbuf[k, n] = jnp.ones((PAIR, width), BF16)

    def surrogate(k):
        ones = jnp.ones((PAIR, lanes_at_once), BF16)
        for c in sends(k):
            c.wait()

        def block(j, carry):
            lanes = pl.ds(pl.multiple_of(j * lanes_at_once, lanes_at_once), lanes_at_once)
            x = xbuf[k, :, :, lanes].reshape((n + 1) * PAIR, lanes_at_once)
            heat_in = xbuf[k, n - 1, :, lanes].astype(F32)
            first, second, scaled = {}, {}, []

            def enter(v):
                first[v] = jnp.dot(w1[v * hid : (v + 1) * hid, :], x, preferred_element_type=F32)

            def middle(v):
                hidden = jnp.concatenate([halves_silu(first.pop(v)), ones], 0)
                second[v] = jnp.dot(w2[...], hidden, preferred_element_type=F32)

            def leave(v):
                hidden = jnp.concatenate([halves_silu(second.pop(v)), ones], 0)
                change = jnp.dot(w3[...], hidden, preferred_element_type=F32)
                last = v * per + per - 1
                heat = heat_in[last : last + 1] + change[FIELDS - 1 :]
                scaled.append(change * jnp.exp(rate_col[...] * jnp.tanh(heat)))

            enter(0)
            for v in range(variants):
                if v + 1 < variants:
                    enter(v + 1)
                middle(v)
                if v > 0:
                    leave(v - 1)
            leave(variants - 1)
            for s in range(n):
                block_out = jnp.concatenate([one[s * per : (s + 1) * per] for one in scaled], 0)
                rbuf[k, s, :, lanes] = block_out.astype(BF16)
            return carry

        lax.fori_loop(0, width // lanes_at_once, block, 0)
        for c in returns(k):
            c.start()

    def finish(k):
        for c in returns(k):
            c.wait()
        low = k * chunk_rows + HALO
        for d in range(n):
            row = (low + 2 * d) * SUB
            s3[row : row + PAIR, :] = s3[row : row + PAIR, :] + ret[k, d].astype(F32)
        for g in range(k * chunk_rows // SUB, (k + 1) * chunk_rows // SUB):

            def lane_block(j, carry, g=g):
                at = pl.multiple_of(j * STEP, STEP)
                slab = s3[(g * SUB + HALO) * SUB : ((g + 1) * SUB + HALO) * SUB, pl.ds(at, STEP)]
                turned = jnp.swapaxes(slab.reshape(SUB, SUB, STEP), 0, 1)
                for p in range(parts):
                    cols = pl.ds(pl.multiple_of(at + p * width, STEP), STEP)
                    for f in range(per):
                        out[f, pl.ds(g * SUB, SUB), cols] = turned[p * per + f]
                return carry

            lax.fori_loop(0, width // STEP, lane_block, 0)

    inner = list(range(1, chunks - 1))
    edge = [k for k in range(chunks) if k not in inner]
    for k in inner:
        stencil(k)
    weights()
    order = inner + edge
    begun = 0
    if inner:
        surrogate(order[0])
        begun = 1
    halo_wait()
    for k in edge:
        stencil(k)
    for i in range(begun, chunks):
        surrogate(order[i])
        if i > 0:
            finish(order[i - 1])
    finish(order[-1])


def on_device(
    n,
    n_space,
    fields,
    zone_ids,
    diffusivity,
    heat_rate,
    weight_in,
    bias_in,
    weight_mid,
    bias_mid,
    weight_out,
    bias_out,
):
    per, rows, columns = fields.shape
    width = columns * per // SUB
    variants = 2 * SUB // per
    lanes_at_once = block_lanes(width)
    hid = weight_mid.shape[0]
    chunks = rows // (2 * n)
    padded = (rows + 2 * HALO) * SUB
    vmem = pl.BlockSpec(memory_space=pltpu.VMEM)
    smem = pl.BlockSpec(memory_space=pltpu.SMEM)
    slab = pltpu.VMEM((padded, width), F32)
    dma = pltpu.SemaphoreType.DMA
    return pl.pallas_call(
        functools.partial(kernel, n, n_space),
        out_shape=jax.ShapeDtypeStruct(fields.shape, F32),
        in_specs=[vmem, vmem, smem] + [vmem] * 7,
        out_specs=vmem,
        scratch_shapes=[slab] * 8
        + [
            pltpu.VMEM((2, 2 * HALO * SUB, width), BF16),
            pltpu.VMEM((2, 2 * HALO * SUB, width), BF16),
            pltpu.VMEM((chunks, n, PAIR, width), BF16),
            pltpu.VMEM((chunks, n + 1, PAIR, width), BF16),
            pltpu.VMEM((chunks, n, PAIR, width), BF16),
            pltpu.VMEM((chunks, n, PAIR, width), BF16),
            pltpu.VMEM((variants * hid, (n + 1) * PAIR), BF16),
            pltpu.VMEM((hid, hid + PAIR), BF16),
            pltpu.VMEM((FIELDS, hid + PAIR), BF16),
            pltpu.VMEM((SUB, 128), F32),
            pltpu.VMEM((FIELDS, lanes_at_once), F32),
            dma((2,)),
            dma((2,)),
            dma((chunks, n)),
            dma((chunks, n)),
            dma((chunks, n)),
            dma((chunks, n)),
            dma((chunks,)),
            dma((chunks,)),
        ],
        compiler_params=pltpu.CompilerParams(
            collective_id=0, has_side_effects=True, vmem_limit_bytes=60 * 1024 * 1024
        ),
        cost_estimate=pl.CostEstimate(
            flops=2 * per * rows * columns // n * hid * (hid + 2 * FIELDS),
            bytes_accessed=9 * per * rows * columns,
            transcendentals=0,
        ),
    )(
        fields,
        zone_ids,
        diffusivity,
        heat_rate,
        weight_in.T,
        bias_in,
        weight_mid,
        bias_mid,
        weight_out,
        bias_out,
    )


def solution(mesh):
    n, n_space = mesh.shape["field"], mesh.shape["space"]
    return jax.shard_map(
        functools.partial(on_device, n, n_space),
        mesh=mesh,
        in_specs=(
            P("field", "space", None),
            P("space", None),
            P("field", None),
            P(),
            P(),
            P(),
            P(),
            P(),
            P(),
            P(),
        ),
        out_specs=P("field", "space", None),
        check_vma=False,
    )
```

profile of v0, /device:TPU:0, one launch (start us, length us, event | category | flops | bytes accessed | tf_op | source)
XLA Modules:
  0.0 79.9 jit_solution(11542711773630624885)
XLA Ops:
  0.0 76.0 %shard_map.100 = f32[4,32,6144]{2,1,0:T(8,128)} custom-call(f32[4,32,6144]{2,1,0:T(8,128)} %fields.1, s32[32,6144]{1,0:T(8,128)} %zones.1, f32[4,8]{1,0:T(4,128)} %diff.1, f32[15]{0:T(128)} %rate.1, bf16[16,384]{1,0:T(8,128)(2,1)} %bitcast.1, f32[384]{0:T(512)} %b_in.1, bf16[384,384]{1,0:T(8,128)(2,1)} %w_mid.1, f32[384]{0:T(512)} %b_mid.1, ...), custom_call_target="tpu_custom_call" | custom-call | flops 62813896704 | bytes 7077888 | tf_op jit(solution)/shard_map/pallas_call | solution.py:432
  76.0 3.9 %copy.12 = f32[4,32,6144]{2,1,0:T(8,128)} copy(f32[4,32,6144]{2,1,0:T(8,128)} %shard_map.100) | data formatting | bytes 6291456
where the time goes:
time: 80.6 us; the launch traced here: 79.9 us
  Pallas kernels  76 us (94%)
  local copies, waits for them, and re-layouts  3.86 us (5%)
    pallas_call x1, Pallas kernels, on_device(): pl.pallas_call(functools.partial(kernel, n, n_space), out_shape=jax.Shape...  76 us
    unnamed x1, local copies, waits for them, and re-layouts  3.86 us

commit v1 on v0

--- a/solution.py
+++ b/solution.py
@@ -20,7 +20,10 @@
 
 
 def block_lanes(width):
-    return 512 if width % 512 == 0 else 256
+    for once, step in ((512, 1024), (512, 512), (256, 768)):
+        if width % step == 0:
+            return once, step
+    return 256, 256
 
 
 def iota2(shape, axis):
@@ -96,7 +99,7 @@
     parts = SUB // per
     width = columns // parts
     variants = 2 * parts
-    lanes_at_once = block_lanes(width)
+    lanes_at_once, lanes_step = block_lanes(width)
     hid = w_mid.shape[0]
     chunks = rows // (2 * n)
     chunk_rows = rows // chunks
@@ -251,28 +254,30 @@
         for c in sends(k):
             c.start()
 
-    def all_copies(src_buf, dst_buf, k, send_sem, recv_sem, local_sem):
+    def all_copies(src_buf, dst_buf, k, send_sem, recv_sem, local_sem, cols=slice(None)):
         copies = []
         for off in range(1, n):
             peer = lax.rem(me + off, n)
             copies.append(
                 pltpu.make_async_remote_copy(
-                    src_ref=src_buf.at[k, peer],
-                    dst_ref=dst_buf.at[k, me],
+                    src_ref=src_buf.at[k, peer, :, cols],
+                    dst_ref=dst_buf.at[k, me, :, cols],
                     send_sem=send_sem.at[k, off],
                     recv_sem=recv_sem.at[k, off],
                     device_id={"field": peer},
                     device_id_type=MESH,
                 )
             )
-        local = pltpu.make_async_copy(src_buf.at[k, me], dst_buf.at[k, me], local_sem.at[k])
+        local = pltpu.make_async_copy(
+            src_buf.at[k, me, :, cols], dst_buf.at[k, me, :, cols], local_sem.at[k]
+        )
         return copies + [local]
 
     def sends(k):
         return all_copies(sbuf, xbuf, k, ssem, rsem, lsem)
 
-    def returns(k):
-        return all_copies(rbuf, ret, k, rssem, rrsem, rlsem)
+    def returns(k, cols=slice(None)):
+        return all_copies(rbuf, ret, k, rssem, rrsem, rlsem, cols)
 
     def halo_wait():
         for slot, row, has in ((0, 0, has_up), (1, rows + HALO, has_down)):
@@ -327,41 +332,52 @@
             c.wait()
 
         def block(j, carry):
-            lanes = pl.ds(pl.multiple_of(j * lanes_at_once, lanes_at_once), lanes_at_once)
-            x = xbuf[k, :, :, lanes].reshape((n + 1) * PAIR, lanes_at_once)
-            heat_in = xbuf[k, n - 1, :, lanes].astype(F32)
+            start = pl.multiple_of(j * lanes_step, lanes_step)
+            subs = lanes_step // lanes_at_once
+            units = [(sub, v) for sub in range(subs) for v in range(variants)]
+            lanes = [
+                pl.ds(pl.multiple_of(start + sub * lanes_at_once, lanes_at_once), lanes_at_once)
+                for sub in range(subs)
+            ]
+            x = [xbuf[k, :, :, at].reshape((n + 1) * PAIR, lanes_at_once) for at in lanes]
+            heat_in = [xbuf[k, n - 1, :, at].astype(F32) for at in lanes]
             first, second, scaled = {}, {}, []
 
-            def enter(v):
-                first[v] = jnp.dot(w1[v * hid : (v + 1) * hid, :], x, preferred_element_type=F32)
-
-            def middle(v):
-                hidden = jnp.concatenate([halves_silu(first.pop(v)), ones], 0)
-                second[v] = jnp.dot(w2[...], hidden, preferred_element_type=F32)
-
-            def leave(v):
-                hidden = jnp.concatenate([halves_silu(second.pop(v)), ones], 0)
+            def enter(u):
+                sub, v = units[u]
+                rows_v = w1[v * hid : (v + 1) * hid, :]
+                first[u] = jnp.dot(rows_v, x[sub], preferred_element_type=F32)
+
+            def middle(u):
+                hidden = jnp.concatenate([halves_silu(first.pop(u)), ones], 0)
+                second[u] = jnp.dot(w2[...], hidden, preferred_element_type=F32)
+
+            def leave(u):
+                sub, v = units[u]
+                hidden = jnp.concatenate([halves_silu(second.pop(u)), ones], 0)
                 change = jnp.dot(w3[...], hidden, preferred_element_type=F32)
                 last = v * per + per - 1
-                heat = heat_in[last : last + 1] + change[FIELDS - 1 :]
+                heat = heat_in[sub][last : last + 1] + change[FIELDS - 1 :]
                 scaled.append(change * jnp.exp(rate_col[...] * jnp.tanh(heat)))
+                if v == variants - 1:
+                    for s in range(n):
+                        pieces = [one[s * per : (s + 1) * per] for one in scaled]
+                        rbuf[k, s, :, lanes[sub]] = jnp.concatenate(pieces, 0).astype(BF16)
+                    scaled.clear()
 
             enter(0)
-            for v in range(variants):
-                if v + 1 < variants:
-                    enter(v + 1)
-                middle(v)
-                if v > 0:
-                    leave(v - 1)
-            leave(variants - 1)
-            for s in range(n):
-                block_out = jnp.concatenate([one[s * per : (s + 1) * per] for one in scaled], 0)
-                rbuf[k, s, :, lanes] = block_out.astype(BF16)
+            for u in range(len(units)):
+                if u + 1 < len(units):
+                    enter(u + 1)
+                middle(u)
+                if u > 0:
+                    leave(u - 1)
+            leave(len(units) - 1)
+            for c in returns(k, pl.ds(start, lanes_step)):
+                c.start()
             return carry
 
-        lax.fori_loop(0, width // lanes_at_once, block, 0)
-        for c in returns(k):
-            c.start()
+        lax.fori_loop(0, width // lanes_step, block, 0)
 
     def finish(k):
         for c in returns(k):
@@ -421,7 +437,7 @@
     per, rows, columns = fields.shape
     width = columns * per // SUB
     variants = 2 * SUB // per
-    lanes_at_once = block_lanes(width)
+    lanes_at_once, lanes_step = block_lanes(width)
     hid = weight_mid.shape[0]
     chunks = rows // (2 * n)
     padded = (rows + 2 * HALO) * SUB

time: 80.6 us -> 76 us (0.943)
  Pallas kernels: 76 us -> 72 us
    pallas_call x1, Pallas kernels: 76 us -> 72 us  [on_device(): pl.pallas_call(functools.partial(kernel, n, n_space), out_shape=jax.Shape...]
where the time goes in v1:
time: 76 us; the launch traced here: 75.9 us
  Pallas kernels  72 us (95%)
  local copies, waits for them, and re-layouts  3.86 us (5%)
    pallas_call x1, Pallas kernels, on_device(): pl.pallas_call(functools.partial(kernel, n, n_space), out_shape=jax.Shape...  72 us
    unnamed x1, local copies, waits for them, and re-layouts  3.86 us

profile of v1, /device:TPU:0, one launch (start us, length us, event | category | flops | bytes accessed | tf_op | source)
XLA Modules:
  0.0 75.9 jit_solution(7794740584534775405)
XLA Ops:
  0.0 72.0 %shard_map.100 = f32[4,32,6144]{2,1,0:T(8,128)} custom-call(f32[4,32,6144]{2,1,0:T(8,128)} %fields.1, s32[32,6144]{1,0:T(8,128)} %zones.1, f32[4,8]{1,0:T(4,128)} %diff.1, f32[15]{0:T(128)} %rate.1, bf16[16,384]{1,0:T(8,128)(2,1)} %bitcast.1, f32[384]{0:T(512)} %b_in.1, bf16[384,384]{1,0:T(8,128)(2,1)} %w_mid.1, f32[384]{0:T(512)} %b_mid.1, ...), custom_call_target="tpu_custom_call" | custom-call | flops 62813896704 | bytes 7077888 | tf_op jit(solution)/shard_map/pallas_call | solution.py:448
  72.0 3.9 %copy.12 = f32[4,32,6144]{2,1,0:T(8,128)} copy(f32[4,32,6144]{2,1,0:T(8,128)} %shard_map.100) | data formatting | bytes 6291456

commit v2 on v1

--- a/solution.py
+++ b/solution.py
@@ -67,14 +67,11 @@
     w_out,
     b_out,
     out,
-    src,
+    states,
     coef,
     face_d,
     face_e,
     rdiag,
-    s1,
-    s2,
-    s3,
     halo_out,
     halo_in,
     sbuf,
@@ -96,6 +93,7 @@
     rlsem,
 ):
     per, rows, columns = fields.shape
+    src, s3 = states.at[0], states.at[SWEEPS]
     parts = SUB // per
     width = columns // parts
     variants = 2 * parts
@@ -202,7 +200,7 @@
     def at_row(r):
         return pl.ds(pl.multiple_of(r * SUB, SUB), SUB)
 
-    def first_row(r, carry):
+    def face_row(r, carry):
         a, b, c = at_row(r - 1), at_row(r), at_row(r + 1)
         mine = coef[b, :]
         down = 0.5 * (mine + coef[c, :])
@@ -214,40 +212,54 @@
             jnp.logical_and(r >= rows + HALO, jnp.logical_not(has_down)),
         )
         scale = jnp.where(outside, 0.0, 1.0).astype(F32)
-        inv = scale / (1.0 + down + up + east + west)
         face_d[b, :] = down
         face_e[b, :] = east
-        rdiag[b, :] = inv
-        v = src[b, :]
-        total = v + down * src[c, :] + up * src[a, :]
+        rdiag[b, :] = scale / (1.0 + down + up + east + west)
+        return carry
+
+    def sweep_row(sweep, weight, r, carry):
+        a, b, c = at_row(r - 1), at_row(r), at_row(r + 1)
+        v = states[sweep, b, :]
+        east = face_e[b, :]
+        total = src[b, :] + face_d[b, :] * states[sweep, c, :] + face_d[a, :] * states[sweep, a, :]
         total = total + east * from_east(v) + from_west(east * v)
-        weight = RELAX_WEIGHTS[0]
-        s1[b, :] = (1.0 - weight) * v + (weight * inv) * total
+        states[sweep + 1, b, :] = (1.0 - weight) * v + (weight * rdiag[b, :]) * total
         return carry
 
-    def later_row(old, new, weight, r, carry):
-        a, b, c = at_row(r - 1), at_row(r), at_row(r + 1)
-        v = old[b, :]
-        east = face_e[b, :]
-        total = src[b, :] + face_d[b, :] * old[c, :] + face_d[a, :] * old[a, :]
-        total = total + east * from_east(v) + from_west(east * v)
-        new[b, :] = (1.0 - weight) * v + (weight * rdiag[b, :]) * total
-        return carry
-
-    steps = (
-        first_row,
-        functools.partial(later_row, s1, s2, RELAX_WEIGHTS[1]),
-        functools.partial(later_row, s2, s3, RELAX_WEIGHTS[2]),
-    )
-    done = [set() for _ in steps]
+    done = [set() for _ in range(SWEEPS)]
+    faced = set()
+
+    def faces(need):
+        need = sorted(set(need) - faced)
+        faced.update(need)
+        for start in [r for r in need if r - 1 not in need]:
+            stop = start
+            while stop in need:
+                stop += 1
+            lax.fori_loop(start, stop, face_row, 0)
+
+    def bounds(k):
+        return k * chunk_rows + HALO, (k + 1) * chunk_rows + HALO
+
+    def sweep_rows(k, sweep):
+        low, high = bounds(k)
+        grow = SWEEPS - 1 - sweep
+        need = sorted(set(range(low - grow, high + grow)) - done[sweep])
+        done[sweep].update(need)
+        return need
 
     def stencil(k):
-        low, high = k * chunk_rows + HALO, (k + 1) * chunk_rows + HALO
-        for number, step in enumerate(steps):
-            grow = SWEEPS - 1 - number
-            need = sorted(set(range(low - grow, high + grow)) - done[number])
-            done[number].update(need)
+        low, high = bounds(k)
+        lowest = max(low - SWEEPS, 0)
+        faces(range(lowest if lowest > 0 else 1, min(high + SWEEPS, rows + 2 * HALO - 1)))
+        for sweep in range(SWEEPS):
+            need = sweep_rows(k, sweep)
+            step = functools.partial(sweep_row, sweep, RELAX_WEIGHTS[sweep])
             lax.fori_loop(need[0], need[-1] + 1, step, 0)
+        send(k)
+
+    def send(k):
+        low = bounds(k)[0]
         for d in range(n):
             row = (low + 2 * d) * SUB
             sbuf[k, d] = s3[row : row + PAIR, :].astype(BF16)
@@ -303,6 +315,8 @@
         @pl.when(has_down)
         def _():
             halo_copy(1).wait_send()
+
+        face_d[0:SUB, :] = 0.5 * (coef[0:SUB, :] + coef[SUB : 2 * SUB, :])
 
     def weights():
         depth = (n + 1) * PAIR
@@ -326,7 +340,7 @@
         for k in range(chunks):
             xbuf[k, n] = jnp.ones((PAIR, width), BF16)
 
-    def surrogate(k):
+    def surrogate(k, beside=None):
         ones = jnp.ones((PAIR, lanes_at_once), BF16)
         for c in sends(k):
             c.wait()
@@ -343,10 +357,10 @@
             heat_in = [xbuf[k, n - 1, :, at].astype(F32) for at in lanes]
             first, second, scaled = {}, {}, []
 
-            def enter(u):
-                sub, v = units[u]
-                rows_v = w1[v * hid : (v + 1) * hid, :]
-                first[u] = jnp.dot(rows_v, x[sub], preferred_element_type=F32)
+            def enter(sub):
+                every = jnp.dot(w1[...], x[sub], preferred_element_type=F32)
+                for v in range(variants):
+                    first[sub * variants + v] = every[v * hid : (v + 1) * hid]
 
             def middle(u):
                 hidden = jnp.concatenate([halves_silu(first.pop(u)), ones], 0)
@@ -367,9 +381,11 @@
 
             enter(0)
             for u in range(len(units)):
-                if u + 1 < len(units):
-                    enter(u + 1)
+                if units[u][1] == variants // 2 and units[u][0] + 1 < subs:
+                    enter(units[u][0] + 1)
                 middle(u)
+                if beside is not None:
+                    beside(j, u)
                 if u > 0:
                     leave(u - 1)
             leave(len(units) - 1)
@@ -402,19 +418,43 @@
 
     inner = list(range(1, chunks - 1))
     edge = [k for k in range(chunks) if k not in inner]
+    order = inner + edge
+    units = lanes_step // lanes_at_once * variants
+    hosted = len(inner) == 2 and width // lanes_step == SWEEPS and chunk_rows == units
     for k in inner:
         stencil(k)
     weights()
-    order = inner + edge
-    begun = 0
-    if inner:
-        surrogate(order[0])
-        begun = 1
     halo_wait()
+    if not hosted:
+        for k in edge:
+            stencil(k)
+        for i, k in enumerate(order):
+            surrogate(k)
+            if i > 0:
+                finish(order[i - 1])
+        finish(order[-1])
+        return
+
     for k in edge:
-        stencil(k)
-    for i in range(begun, chunks):
-        surrogate(order[i])
+        low, high = bounds(k)
+        faces(range(max(low - 2, 1), min(high + 2, rows + 2 * HALO - 1)))
+
+    def beside(k):
+        starts = [sweep_rows(k, sweep) for sweep in range(SWEEPS)]
+        stride = starts[1][0] - starts[0][0]
+        start = starts[0][0]
+
+        def row(j, u):
+            weight = jnp.where(j == 0, RELAX_WEIGHTS[0], RELAX_WEIGHTS[1])
+            weight = jnp.where(j == 2, RELAX_WEIGHTS[2], weight).astype(F32)
+            sweep_row(j, weight, start + stride * j + u, 0)
+
+        return row
+
+    for i, k in enumerate(order):
+        surrogate(k, beside(edge[i]) if i < len(edge) else None)
+        if i < len(edge):
+            send(edge[i])
         if i > 0:
             finish(order[i - 1])
     finish(order[-1])
@@ -450,7 +490,8 @@
         out_shape=jax.ShapeDtypeStruct(fields.shape, F32),
         in_specs=[vmem, vmem, smem] + [vmem] * 7,
         out_specs=vmem,
-        scratch_shapes=[slab] * 8
+        scratch_shapes=[pltpu.VMEM((SWEEPS + 1, padded, width), F32)]
+        + [slab] * 4
         + [
             pltpu.VMEM((2, 2 * HALO * SUB, width), BF16),
             pltpu.VMEM((2, 2 * HALO * SUB, width), BF16),

time: 76 us -> 76.5 us (level); the launches traced: 75.9 us -> 75.5 us
  no operation moved by 1% of the time
where the time goes in v2:
time: 76.5 us; the launch traced here: 75.5 us
  Pallas kernels  71.6 us (94%)
  local copies, waits for them, and re-layouts  3.86 us (5%)
    pallas_call x1, Pallas kernels, on_device(): pl.pallas_call(functools.partial(kernel, n, n_space), out_shape=jax.Shape...  71.6 us
    unnamed x1, local copies, waits for them, and re-layouts  3.86 us

profile of v2, /device:TPU:0, one launch (start us, length us, event | category | flops | bytes accessed | tf_op | source)
XLA Modules:
  0.0 75.5 jit_solution(14602494469233293567)
XLA Ops:
  0.0 71.6 %shard_map.100 = f32[4,32,6144]{2,1,0:T(8,128)} custom-call(f32[4,32,6144]{2,1,0:T(8,128)} %fields.1, s32[32,6144]{1,0:T(8,128)} %zones.1, f32[4,8]{1,0:T(4,128)} %diff.1, f32[15]{0:T(128)} %rate.1, bf16[16,384]{1,0:T(8,128)(2,1)} %bitcast.1, f32[384]{0:T(512)} %b_in.1, bf16[384,384]{1,0:T(8,128)(2,1)} %w_mid.1, f32[384]{0:T(512)} %b_mid.1, ...), custom_call_target="tpu_custom_call" | custom-call | flops 62813896704 | bytes 7077888 | tf_op jit(solution)/shard_map/pallas_call | solution.py:488
  71.6 3.9 %copy.12 = f32[4,32,6144]{2,1,0:T(8,128)} copy(f32[4,32,6144]{2,1,0:T(8,128)} %shard_map.100) | data formatting | bytes 6291456

commit v3 on v2

--- a/solution.py
+++ b/solution.py
@@ -424,6 +424,8 @@
     for k in inner:
         stencil(k)
     weights()
+    if hosted:
+        surrogate(order[0])
     halo_wait()
     if not hosted:
         for k in edge:
@@ -451,12 +453,12 @@
 
         return row
 
-    for i, k in enumerate(order):
-        surrogate(k, beside(edge[i]) if i < len(edge) else None)
-        if i < len(edge):
-            send(edge[i])
-        if i > 0:
-            finish(order[i - 1])
+    stencil(edge[0])
+    for i, k in enumerate(order[1:]):
+        surrogate(k, beside(edge[1]) if i == 0 else None)
+        if i == 0:
+            send(edge[1])
+        finish(order[i])
     finish(order[-1])
 
 

time: 76.5 us -> 78.3 us (1.024); the launches traced: 75.5 us -> 78.2 us
  Pallas kernels: 71.6 us -> 74.3 us
    pallas_call x1, Pallas kernels: 71.6 us -> 74.3 us  [on_device(): pl.pallas_call(functools.partial(kernel, n, n_space), out_shape=jax.Shape...]
where the time goes in v3:
time: 78.3 us; the launch traced here: 78.2 us
  Pallas kernels  74.3 us (95%)
  local copies, waits for them, and re-layouts  3.86 us (5%)
    pallas_call x1, Pallas kernels, on_device(): pl.pallas_call(functools.partial(kernel, n, n_space), out_shape=jax.Shape...  74.3 us
    unnamed x1, local copies, waits for them, and re-layouts  3.86 us

profile of v3, /device:TPU:0, one launch (start us, length us, event | category | flops | bytes accessed | tf_op | source)
XLA Modules:
  0.0 78.2 jit_solution(18294328049976391875)
XLA Ops:
  0.0 74.3 %shard_map.100 = f32[4,32,6144]{2,1,0:T(8,128)} custom-call(f32[4,32,6144]{2,1,0:T(8,128)} %fields.1, s32[32,6144]{1,0:T(8,128)} %zones.1, f32[4,8]{1,0:T(4,128)} %diff.1, f32[15]{0:T(128)} %rate.1, bf16[16,384]{1,0:T(8,128)(2,1)} %bitcast.1, f32[384]{0:T(512)} %b_in.1, bf16[384,384]{1,0:T(8,128)(2,1)} %w_mid.1, f32[384]{0:T(512)} %b_mid.1, ...), custom_call_target="tpu_custom_call" | custom-call | flops 62813896704 | bytes 7077888 | tf_op jit(solution)/shard_map/pallas_call | solution.py:490
  74.3 3.9 %copy.12 = f32[4,32,6144]{2,1,0:T(8,128)} copy(f32[4,32,6144]{2,1,0:T(8,128)} %shard_map.100) | data formatting | bytes 6291456

commit v4 on v2

--- a/solution.py
+++ b/solution.py
@@ -357,10 +357,10 @@
             heat_in = [xbuf[k, n - 1, :, at].astype(F32) for at in lanes]
             first, second, scaled = {}, {}, []
 
-            def enter(sub):
-                every = jnp.dot(w1[...], x[sub], preferred_element_type=F32)
-                for v in range(variants):
-                    first[sub * variants + v] = every[v * hid : (v + 1) * hid]
+            def enter(u):
+                sub, v = units[u]
+                rows_v = w1[v * hid : (v + 1) * hid, :]
+                first[u] = jnp.dot(rows_v, x[sub], preferred_element_type=F32)
 
             def middle(u):
                 hidden = jnp.concatenate([halves_silu(first.pop(u)), ones], 0)
@@ -381,8 +381,8 @@
 
             enter(0)
             for u in range(len(units)):
-                if units[u][1] == variants // 2 and units[u][0] + 1 < subs:
-                    enter(units[u][0] + 1)
+                if u + 1 < len(units):
+                    enter(u + 1)
                 middle(u)
                 if beside is not None:
                     beside(j, u)

time: 76.5 us -> 74.4 us (0.973)
  Pallas kernels: 71.6 us -> 69.6 us
    pallas_call x1, Pallas kernels: 71.6 us -> 69.6 us  [on_device(): pl.pallas_call(functools.partial(kernel, n, n_space), out_shape=jax.Shape...]
where the time goes in v4:
time: 74.4 us; the launch traced here: 73.4 us
  Pallas kernels  69.6 us (94%)
  local copies, waits for them, and re-layouts  3.86 us (5%)
    pallas_call x1, Pallas kernels, on_device(): pl.pallas_call(functools.partial(kernel, n, n_space), out_shape=jax.Shape...  69.6 us
    unnamed x1, local copies, waits for them, and re-layouts  3.86 us

profile of v4, /device:TPU:0, one launch (start us, length us, event | category | flops | bytes accessed | tf_op | source)
XLA Modules:
  0.0 73.4 jit_solution(146216089011662055)
XLA Ops:
  0.0 69.6 %shard_map.100 = f32[4,32,6144]{2,1,0:T(8,128)} custom-call(f32[4,32,6144]{2,1,0:T(8,128)} %fields.1, s32[32,6144]{1,0:T(8,128)} %zones.1, f32[4,8]{1,0:T(4,128)} %diff.1, f32[15]{0:T(128)} %rate.1, bf16[16,384]{1,0:T(8,128)(2,1)} %bitcast.1, f32[384]{0:T(512)} %b_in.1, bf16[384,384]{1,0:T(8,128)(2,1)} %w_mid.1, f32[384]{0:T(512)} %b_mid.1, ...), custom_call_target="tpu_custom_call" | custom-call | flops 62813896704 | bytes 7077888 | tf_op jit(solution)/shard_map/pallas_call | solution.py:488
  69.6 3.9 %copy.12 = f32[4,32,6144]{2,1,0:T(8,128)} copy(f32[4,32,6144]{2,1,0:T(8,128)} %shard_map.100) | data formatting | bytes 6291456
